TPU v7x, 128 devices: a whole 4x4x4 slice. The times are simulated.
128 devices in a mesh: outer: 16 (over y_hi, z, core), inner: 8 (over x, y_lo).
Axes of the slice: x: 4, y: 4 (y_hi: 2, y_lo: 2; y = y_hi * 2 + y_lo), z: 4, core: 2. Of those that a mesh axis runs over, the one named last changes fastest.
Arguments:
- queries: bfloat16 [16384, 4096], P(('outer', 'inner')), may hold values from -16 to 16
- keys: bfloat16 [16384, 512], P(('outer', 'inner')), may hold values from -6 to 6
- values: bfloat16 [16384, 512], P(('outer', 'inner')), may hold values from -6 to 6
- block_pos: int32 [256], replicated, may hold values from 0 to 255, as said below
- cache_slot: int32 [256], replicated, may hold values from 0 to 255, each once
Outputs:
- attended: bfloat16 [16384, 4096], P(('outer', 'inner'))
- cached_keys: bfloat16 [16384, 512], P(('outer', 'inner'))
- cached_values: bfloat16 [16384, 512], P(('outer', 'inner'))
Inputs may be any that keep to these rules, and one draw needn't show every extreme that they name: block_pos is a permutation; block_pos[2 j] < 128 and block_pos[2 j + 1] = 255 - block_pos[2 j]. `cache_slot`: a permutation.
All inputs are finite; a program needn't handle non-finite values.
Results may differ from a plain program's by a relative error of at most 0.007.
Values may be sent and summed in bfloat16 or wider, within the bound.
A program may use at most 128 MiB of HBM per device.

v0:
```python
import math

import jax
import jax.numpy as jnp
from jax import lax
from jax.sharding import PartitionSpec as P

LOCAL_KEY_HEADS = 4
HEAD_DIMENSION = 128


def shifted(array, axis, by):
    devices = lax.axis_size(axis)
    return lax.ppermute(array, axis, [(i, (i + by) % devices) for i in range(devices)])


def block_positions(block_pos, first_row, count_of_rows, half_block_rows):
    global_rows = first_row + jnp.arange(count_of_rows, dtype=jnp.int32)
    half_index = global_rows // half_block_rows
    one_hot = half_index[:, None] == jnp.arange(block_pos.shape[0], dtype=jnp.int32)[None, :]
    block_start = jnp.sum(jnp.where(one_hot, block_pos[None, :], 0), axis=1)
    return block_start * half_block_rows + global_rows % half_block_rows


def attend(carried, query_row_block, query_pos, key_row_block, value_row_block, key_pos):
    running_maximum, running_sum, running_totals = carried
    count_of_rows = query_row_block.shape[0]
    group_width = query_row_block.shape[1] // (LOCAL_KEY_HEADS * HEAD_DIMENSION)
    query_head_rows = query_row_block.reshape(
        count_of_rows, LOCAL_KEY_HEADS, group_width, HEAD_DIMENSION
    )
    key_head_rows = key_row_block.reshape(-1, LOCAL_KEY_HEADS, HEAD_DIMENSION)
    value_head_rows = value_row_block.reshape(-1, LOCAL_KEY_HEADS, HEAD_DIMENSION)
    scores = jnp.einsum(
        "rhgd,khd->rhgk", query_head_rows, key_head_rows, preferred_element_type=jnp.float32
    ) * (1.0 / math.sqrt(HEAD_DIMENSION))
    visible = (key_pos[None, :] <= query_pos[:, None])[:, None, None, :]
    block_max = jnp.max(jnp.where(visible, scores, -1e30), axis=3)
    prior_maximum = running_maximum.reshape(count_of_rows, LOCAL_KEY_HEADS, group_width)
    new_max = jnp.maximum(prior_maximum, block_max)
    rescale_factor = jnp.exp(prior_maximum - new_max)
    attention_weights = jnp.where(visible, jnp.exp(scores - new_max[..., None]), 0.0)
    updated_sum = running_sum.reshape(
        count_of_rows, LOCAL_KEY_HEADS, group_width
    ) * rescale_factor + jnp.sum(attention_weights, axis=3)
    weighted_values = jnp.einsum(
        "rhgk,khd->rhgd",
        attention_weights.astype(jnp.bfloat16),
        value_head_rows,
        preferred_element_type=jnp.float32,
    )
    updated_totals = (
        running_totals.reshape(count_of_rows, LOCAL_KEY_HEADS, group_width, HEAD_DIMENSION)
        * rescale_factor[..., None]
        + weighted_values
    )
    return (
        new_max.reshape(count_of_rows, -1),
        updated_sum.reshape(count_of_rows, -1),
        updated_totals.reshape(count_of_rows, -1),
    )


def capture_one(old_rows, row_block, base_row, half_block_rows):
    count_of_rows = row_block.shape[0]
    inside = (base_row >= 0) & (base_row < count_of_rows)
    start = jnp.clip(base_row, 0, count_of_rows - half_block_rows)
    picked = lax.dynamic_slice_in_dim(row_block, start, half_block_rows, 0)
    return jnp.where(inside, picked, old_rows)


def capture(caches, key_row_block, value_row_block, first_row, sources, half_block_rows):
    kept = []
    for slot_index in range(2):
        base_row = sources[slot_index] * half_block_rows - first_row
        kept.append(capture_one(caches[2 * slot_index], key_row_block, base_row, half_block_rows))
        kept.append(
            capture_one(caches[2 * slot_index + 1], value_row_block, base_row, half_block_rows)
        )
    return tuple(kept)


def local(queries, keys, values, block_pos, cache_slot):
    tok_rows, query_width = queries.shape
    kv_width = keys.shape[1]
    half_block_rows = tok_rows // 2
    inner_count = lax.axis_size("inner")
    outer_count = lax.axis_size("outer")
    outer_index = lax.axis_index("outer")
    self_index = outer_index * inner_count + lax.axis_index("inner")
    block_count = block_pos.shape[0]
    query_pos = block_positions(block_pos, self_index * tok_rows, tok_rows, half_block_rows)
    my_slots = self_index * 2 + jnp.arange(2, dtype=jnp.int32)
    sources = jnp.sum(
        jnp.where(
            cache_slot[None, :] == my_slots[:, None],
            jnp.arange(block_count, dtype=jnp.int32)[None, :],
            0,
        ),
        axis=1,
    )
    head_count = query_width // HEAD_DIMENSION
    early_queries = queries[:half_block_rows]
    late_queries = queries[half_block_rows:]
    early_query_pos = query_pos[:half_block_rows]
    late_query_pos = query_pos[half_block_rows:]

    def empty_half():
        return (
            jnp.full((half_block_rows, head_count), -1e30, jnp.float32),
            jnp.zeros((half_block_rows, head_count), jnp.float32),
            jnp.zeros((half_block_rows, query_width), jnp.float32),
        )

    empty_cache = jnp.zeros((half_block_rows, kv_width), jnp.bfloat16)
    start_state = (empty_half(), empty_half(), (empty_cache, empty_cache, empty_cache, empty_cache))

    def split_rows(carried, key_row_block, value_row_block, key_pos):
        key_halves = key_row_block.reshape(-1, 2, half_block_rows, kv_width)
        value_halves = value_row_block.reshape(-1, 2, half_block_rows, kv_width)
        early_keys = key_halves[:, 0].reshape(-1, kv_width)
        early_values = value_halves[:, 0].reshape(-1, kv_width)
        early_pos = key_pos.reshape(-1, 2, half_block_rows)[:, 0].reshape(-1)
        first_half = attend(
            carried[0], early_queries, early_query_pos, early_keys, early_values, early_pos
        )
        second_half = attend(
            carried[1], late_queries, late_query_pos, key_row_block, value_row_block, key_pos
        )
        return (first_half, second_half)

    def visit(carried, key_row_block, value_row_block, first_row, attend_rows):
        key_pos = block_positions(block_pos, first_row, key_row_block.shape[0], half_block_rows)
        first_half, second_half = attend_rows(carried, key_row_block, value_row_block, key_pos)
        caches = capture(
            carried[2], key_row_block, value_row_block, first_row, sources, half_block_rows
        )
        return (first_half, second_half, caches)

    local_pair = jnp.stack([keys, values])
    group_span = tok_rows * inner_count
    group_pair = lax.all_gather(local_pair, "inner", axis=1, tiled=True)
    own_state = visit(
        start_state, group_pair[0], group_pair[1], outer_index * group_span, split_rows
    )

    def one_way(step_index, carry_all):
        carried, moving = carry_all
        moving = shifted(moving, "outer", 1)
        carried = visit(
            carried,
            moving[0],
            moving[1],
            (outer_index - step_index) % outer_count * group_span,
            split_rows,
        )
        return (carried, moving)

    final, moving = lax.fori_loop(1, outer_count, one_way, (own_state, group_pair))
    first_half, second_half, caches = final

    def finish(half_state):
        return (
            (
                half_state[2].reshape(half_block_rows, head_count, HEAD_DIMENSION)
                / half_state[1][..., None]
            )
            .reshape(half_block_rows, query_width)
            .astype(jnp.bfloat16)
        )

    attended = jnp.concatenate([finish(first_half), finish(second_half)], axis=0)
    cached_keys = jnp.concatenate([caches[0], caches[2]], axis=0)
    cached_values = jnp.concatenate([caches[1], caches[3]], axis=0)
    return (attended, cached_keys, cached_values)


def solution(mesh):
    return jax.shard_map(
        local,
        mesh=mesh,
        in_specs=(
            P(("outer", "inner"), None),
            P(("outer", "inner"), None),
            P(("outer", "inner"), None),
            P(),
            P(),
        ),
        out_specs=(
            P(("outer", "inner"), None),
            P(("outer", "inner"), None),
            P(("outer", "inner"), None),
        ),
        check_vma=False,
    )
```

profile of v0, /device:TPU:0, one launch (start us, length us, event | category | flops | bytes accessed | tf_op | source)
XLA Modules:
  0.0 1067.2 jit_solution(2827979068909816853)
XLA Ops:
  20.3 43.5 %all-gather.2.cloned.1.call-done = bf16[2,1024,512]{2,1,0:T(8,128)(2,1)} async-done(((bf16[2,128,512]{2,1,0:T(8,128)(2,1)}), bf16[2,1024,512]{2,1,0:T(8,128)(2,1)}) %all-gather.2.cloned.1.call-update) | async-done | bytes 2097168 | tf_op jit(solution)/shard_map/all_gather | solution.py:142
  89.2 964.0 %while.36 = (s32[]{:T(128)}, f32[64,32]{0,1:T(8,128)S(1)}, f32[64,32]{0,1:T(8,128)}, f32[64,4096]{1,0:T(8,128)}, f32[64,32]{0,1:T(8,128)S(1)}, /*index=5*/f32[64...) while((s32[]{:T(128)}, f32[64,32]{0,1:T(8,128)S(1)}, ...), condition=%wide.region_13.14_spmd, body=%wide.region_7.13_spmd.sunk | while | flops 1644199936 | bytes 118046768 | solution.py:159
  98.3 20.2 %collective-permute-done = bf16[2,1024,512]{2,1,0:T(8,128)(2,1)S(1)} collective-permute-done((bf16[2,1024,512]{2,1,0:T(8,128)(2,1)}, bf16[2,1024,512]{2,1,0:T(8,128)(2,1)S(1)}, u32[]{:S(2)}, u32[]{:S(2)}) %collective-permute-start) | collective-permute-done | bytes 2097184 | tf_op jit(solution)/shard_map/while/body/eval_jaxpr/ppermute | solution.py:14
  129.9 4.1 fusion.140
  162.6 20.2 %collective-permute-done = bf16[2,1024,512]{2,1,0:T(8,128)(2,1)S(1)} collective-permute-done((bf16[2,1024,512]{2,1,0:T(8,128)(2,1)}, bf16[2,1024,512]{2,1,0:T(8,128)(2,1)S(1)}, u32[]{:S(2)}, u32[]{:S(2)}) %collective-permute-start) | collective-permute-done | bytes 2097184 | tf_op jit(solution)/shard_map/while/body/eval_jaxpr/ppermute | solution.py:14
  194.2 4.1 fusion.140
  226.9 20.2 %collective-permute-done = bf16[2,1024,512]{2,1,0:T(8,128)(2,1)S(1)} collective-permute-done((bf16[2,1024,512]{2,1,0:T(8,128)(2,1)}, bf16[2,1024,512]{2,1,0:T(8,128)(2,1)S(1)}, u32[]{:S(2)}, u32[]{:S(2)}) %collective-permute-start) | collective-permute-done | bytes 2097184 | tf_op jit(solution)/shard_map/while/body/eval_jaxpr/ppermute | solution.py:14
  258.5 4.1 fusion.140
  291.1 20.2 %collective-permute-done = bf16[2,1024,512]{2,1,0:T(8,128)(2,1)S(1)} collective-permute-done((bf16[2,1024,512]{2,1,0:T(8,128)(2,1)}, bf16[2,1024,512]{2,1,0:T(8,128)(2,1)S(1)}, u32[]{:S(2)}, u32[]{:S(2)}) %collective-permute-start) | collective-permute-done | bytes 2097184 | tf_op jit(solution)/shard_map/while/body/eval_jaxpr/ppermute | solution.py:14
  322.7 4.1 fusion.140
  355.4 20.2 %collective-permute-done = bf16[2,1024,512]{2,1,0:T(8,128)(2,1)S(1)} collective-permute-done((bf16[2,1024,512]{2,1,0:T(8,128)(2,1)}, bf16[2,1024,512]{2,1,0:T(8,128)(2,1)S(1)}, u32[]{:S(2)}, u32[]{:S(2)}) %collective-permute-start) | collective-permute-done | bytes 2097184 | tf_op jit(solution)/shard_map/while/body/eval_jaxpr/ppermute | solution.py:14
  387.0 4.1 fusion.140
  419.6 20.2 %collective-permute-done = bf16[2,1024,512]{2,1,0:T(8,128)(2,1)S(1)} collective-permute-done((bf16[2,1024,512]{2,1,0:T(8,128)(2,1)}, bf16[2,1024,512]{2,1,0:T(8,128)(2,1)S(1)}, u32[]{:S(2)}, u32[]{:S(2)}) %collective-permute-start) | collective-permute-done | bytes 2097184 | tf_op jit(solution)/shard_map/while/body/eval_jaxpr/ppermute | solution.py:14
  451.2 4.1 fusion.140
  483.9 20.2 %collective-permute-done = bf16[2,1024,512]{2,1,0:T(8,128)(2,1)S(1)} collective-permute-done((bf16[2,1024,512]{2,1,0:T(8,128)(2,1)}, bf16[2,1024,512]{2,1,0:T(8,128)(2,1)S(1)}, u32[]{:S(2)}, u32[]{:S(2)}) %collective-permute-start) | collective-permute-done | bytes 2097184 | tf_op jit(solution)/shard_map/while/body/eval_jaxpr/ppermute | solution.py:14
  515.5 4.1 fusion.140
  548.2 20.2 %collective-permute-done = bf16[2,1024,512]{2,1,0:T(8,128)(2,1)S(1)} collective-permute-done((bf16[2,1024,512]{2,1,0:T(8,128)(2,1)}, bf16[2,1024,512]{2,1,0:T(8,128)(2,1)S(1)}, u32[]{:S(2)}, u32[]{:S(2)}) %collective-permute-start) | collective-permute-done | bytes 2097184 | tf_op jit(solution)/shard_map/while/body/eval_jaxpr/ppermute | solution.py:14
  579.7 4.1 fusion.140
  612.4 20.2 %collective-permute-done = bf16[2,1024,512]{2,1,0:T(8,128)(2,1)S(1)} collective-permute-done((bf16[2,1024,512]{2,1,0:T(8,128)(2,1)}, bf16[2,1024,512]{2,1,0:T(8,128)(2,1)S(1)}, u32[]{:S(2)}, u32[]{:S(2)}) %collective-permute-start) | collective-permute-done | bytes 2097184 | tf_op jit(solution)/shard_map/while/body/eval_jaxpr/ppermute | solution.py:14
  644.0 4.1 fusion.140
  676.7 20.2 %collective-permute-done = bf16[2,1024,512]{2,1,0:T(8,128)(2,1)S(1)} collective-permute-done((bf16[2,1024,512]{2,1,0:T(8,128)(2,1)}, bf16[2,1024,512]{2,1,0:T(8,128)(2,1)S(1)}, u32[]{:S(2)}, u32[]{:S(2)}) %collective-permute-start) | collective-permute-done | bytes 2097184 | tf_op jit(solution)/shard_map/while/body/eval_jaxpr/ppermute | solution.py:14
  708.2 4.1 fusion.140
  740.9 20.2 %collective-permute-done = bf16[2,1024,512]{2,1,0:T(8,128)(2,1)S(1)} collective-permute-done((bf16[2,1024,512]{2,1,0:T(8,128)(2,1)}, bf16[2,1024,512]{2,1,0:T(8,128)(2,1)S(1)}, u32[]{:S(2)}, u32[]{:S(2)}) %collective-permute-start) | collective-permute-done | bytes 2097184 | tf_op jit(solution)/shard_map/while/body/eval_jaxpr/ppermute | solution.py:14
  772.5 4.1 fusion.140
  805.2 20.2 %collective-permute-done = bf16[2,1024,512]{2,1,0:T(8,128)(2,1)S(1)} collective-permute-done((bf16[2,1024,512]{2,1,0:T(8,128)(2,1)}, bf16[2,1024,512]{2,1,0:T(8,128)(2,1)S(1)}, u32[]{:S(2)}, u32[]{:S(2)}) %collective-permute-start) | collective-permute-done | bytes 2097184 | tf_op jit(solution)/shard_map/while/body/eval_jaxpr/ppermute | solution.py:14
  836.7 4.1 fusion.140
  869.4 20.2 %collective-permute-done = bf16[2,1024,512]{2,1,0:T(8,128)(2,1)S(1)} collective-permute-done((bf16[2,1024,512]{2,1,0:T(8,128)(2,1)}, bf16[2,1024,512]{2,1,0:T(8,128)(2,1)S(1)}, u32[]{:S(2)}, u32[]{:S(2)}) %collective-permute-start) | collective-permute-done | bytes 2097184 | tf_op jit(solution)/shard_map/while/body/eval_jaxpr/ppermute | solution.py:14
  901.0 4.1 fusion.140
  933.7 20.2 %collective-permute-done = bf16[2,1024,512]{2,1,0:T(8,128)(2,1)S(1)} collective-permute-done((bf16[2,1024,512]{2,1,0:T(8,128)(2,1)}, bf16[2,1024,512]{2,1,0:T(8,128)(2,1)S(1)}, u32[]{:S(2)}, u32[]{:S(2)}) %collective-permute-start) | collective-permute-done | bytes 2097184 | tf_op jit(solution)/shard_map/while/body/eval_jaxpr/ppermute | solution.py:14
  965.3 4.1 fusion.140
  998.0 20.2 %collective-permute-done = bf16[2,1024,512]{2,1,0:T(8,128)(2,1)S(1)} collective-permute-done((bf16[2,1024,512]{2,1,0:T(8,128)(2,1)}, bf16[2,1024,512]{2,1,0:T(8,128)(2,1)S(1)}, u32[]{:S(2)}, u32[]{:S(2)}) %collective-permute-start) | collective-permute-done | bytes 2097184 | tf_op jit(solution)/shard_map/while/body/eval_jaxpr/ppermute | solution.py:14
  1029.6 4.1 fusion.140
  (1140 shorter events, 639.1 us)
Async XLA Ops:
  7.2 56.7 %all-gather.2.cloned.1.call-start = ((), (), s32[]{:S(2)}) async-start(), calls=%async_computation | async-start | bytes 2359296 | tf_op jit(solution)/shard_map/all_gather | solution.py:142
  89.2 29.3 %collective-permute-start = (bf16[2,1024,512]{2,1,0:T(8,128)(2,1)}, bf16[2,1024,512]{2,1,0:T(8,128)(2,1)S(1)}, u32[]{:S(2)}, u32[]{:S(2)}) collective-permute-start(bf16[2,1024,512]{2,1,0:T(8,128)(2,1)} %get-tuple-element.831), channel_id=1, source_target_pairs={{0,8},{8,16},{16,24},{24,32},{32,40},{40,48},{48,56},{56,64},{64,7... | collective-permute-start | bytes 6291464 | tf_op jit(solution)/shard_map/while/body/eval_jaxpr/ppermute | solution.py:14
  90.5 5.1 copy-start.3
  153.5 29.3 %collective-permute-start = (bf16[2,1024,512]{2,1,0:T(8,128)(2,1)}, bf16[2,1024,512]{2,1,0:T(8,128)(2,1)S(1)}, u32[]{:S(2)}, u32[]{:S(2)}) collective-permute-start(bf16[2,1024,512]{2,1,0:T(8,128)(2,1)} %get-tuple-element.831), channel_id=1, source_target_pairs={{0,8},{8,16},{16,24},{24,32},{32,40},{40,48},{48,56},{56,64},{64,7... | collective-permute-start | bytes 6291464 | tf_op jit(solution)/shard_map/while/body/eval_jaxpr/ppermute | solution.py:14
  154.8 5.1 copy-start.3
  217.8 29.3 %collective-permute-start = (bf16[2,1024,512]{2,1,0:T(8,128)(2,1)}, bf16[2,1024,512]{2,1,0:T(8,128)(2,1)S(1)}, u32[]{:S(2)}, u32[]{:S(2)}) collective-permute-start(bf16[2,1024,512]{2,1,0:T(8,128)(2,1)} %get-tuple-element.831), channel_id=1, source_target_pairs={{0,8},{8,16},{16,24},{24,32},{32,40},{40,48},{48,56},{56,64},{64,7... | collective-permute-start | bytes 6291464 | tf_op jit(solution)/shard_map/while/body/eval_jaxpr/ppermute | solution.py:14
  219.1 5.1 copy-start.3
  282.1 29.3 %collective-permute-start = (bf16[2,1024,512]{2,1,0:T(8,128)(2,1)}, bf16[2,1024,512]{2,1,0:T(8,128)(2,1)S(1)}, u32[]{:S(2)}, u32[]{:S(2)}) collective-permute-start(bf16[2,1024,512]{2,1,0:T(8,128)(2,1)} %get-tuple-element.831), channel_id=1, source_target_pairs={{0,8},{8,16},{16,24},{24,32},{32,40},{40,48},{48,56},{56,64},{64,7... | collective-permute-start | bytes 6291464 | tf_op jit(solution)/shard_map/while/body/eval_jaxpr/ppermute | solution.py:14
  283.4 5.1 copy-start.3
  346.3 29.3 %collective-permute-start = (bf16[2,1024,512]{2,1,0:T(8,128)(2,1)}, bf16[2,1024,512]{2,1,0:T(8,128)(2,1)S(1)}, u32[]{:S(2)}, u32[]{:S(2)}) collective-permute-start(bf16[2,1024,512]{2,1,0:T(8,128)(2,1)} %get-tuple-element.831), channel_id=1, source_target_pairs={{0,8},{8,16},{16,24},{24,32},{32,40},{40,48},{48,56},{56,64},{64,7... | collective-permute-start | bytes 6291464 | tf_op jit(solution)/shard_map/while/body/eval_jaxpr/ppermute | solution.py:14
  347.6 5.1 copy-start.3
  410.6 29.3 %collective-permute-start = (bf16[2,1024,512]{2,1,0:T(8,128)(2,1)}, bf16[2,1024,512]{2,1,0:T(8,128)(2,1)S(1)}, u32[]{:S(2)}, u32[]{:S(2)}) collective-permute-start(bf16[2,1024,512]{2,1,0:T(8,128)(2,1)} %get-tuple-element.831), channel_id=1, source_target_pairs={{0,8},{8,16},{16,24},{24,32},{32,40},{40,48},{48,56},{56,64},{64,7... | collective-permute-start | bytes 6291464 | tf_op jit(solution)/shard_map/while/body/eval_jaxpr/ppermute | solution.py:14
  411.9 5.1 copy-start.3
  474.8 29.3 %collective-permute-start = (bf16[2,1024,512]{2,1,0:T(8,128)(2,1)}, bf16[2,1024,512]{2,1,0:T(8,128)(2,1)S(1)}, u32[]{:S(2)}, u32[]{:S(2)}) collective-permute-start(bf16[2,1024,512]{2,1,0:T(8,128)(2,1)} %get-tuple-element.831), channel_id=1, source_target_pairs={{0,8},{8,16},{16,24},{24,32},{32,40},{40,48},{48,56},{56,64},{64,7... | collective-permute-start | bytes 6291464 | tf_op jit(solution)/shard_map/while/body/eval_jaxpr/ppermute | solution.py:14
  476.1 5.1 copy-start.3
  539.1 29.3 %collective-permute-start = (bf16[2,1024,512]{2,1,0:T(8,128)(2,1)}, bf16[2,1024,512]{2,1,0:T(8,128)(2,1)S(1)}, u32[]{:S(2)}, u32[]{:S(2)}) collective-permute-start(bf16[2,1024,512]{2,1,0:T(8,128)(2,1)} %get-tuple-element.831), channel_id=1, source_target_pairs={{0,8},{8,16},{16,24},{24,32},{32,40},{40,48},{48,56},{56,64},{64,7... | collective-permute-start | bytes 6291464 | tf_op jit(solution)/shard_map/while/body/eval_jaxpr/ppermute | solution.py:14
  540.4 5.1 copy-start.3
  603.3 29.3 %collective-permute-start = (bf16[2,1024,512]{2,1,0:T(8,128)(2,1)}, bf16[2,1024,512]{2,1,0:T(8,128)(2,1)S(1)}, u32[]{:S(2)}, u32[]{:S(2)}) collective-permute-start(bf16[2,1024,512]{2,1,0:T(8,128)(2,1)} %get-tuple-element.831), channel_id=1, source_target_pairs={{0,8},{8,16},{16,24},{24,32},{32,40},{40,48},{48,56},{56,64},{64,7... | collective-permute-start | bytes 6291464 | tf_op jit(solution)/shard_map/while/body/eval_jaxpr/ppermute | solution.py:14
  604.6 5.1 copy-start.3
  667.6 29.3 %collective-permute-start = (bf16[2,1024,512]{2,1,0:T(8,128)(2,1)}, bf16[2,1024,512]{2,1,0:T(8,128)(2,1)S(1)}, u32[]{:S(2)}, u32[]{:S(2)}) collective-permute-start(bf16[2,1024,512]{2,1,0:T(8,128)(2,1)} %get-tuple-element.831), channel_id=1, source_target_pairs={{0,8},{8,16},{16,24},{24,32},{32,40},{40,48},{48,56},{56,64},{64,7... | collective-permute-start | bytes 6291464 | tf_op jit(solution)/shard_map/while/body/eval_jaxpr/ppermute | solution.py:14
  668.9 5.1 copy-start.3
  731.9 29.3 %collective-permute-start = (bf16[2,1024,512]{2,1,0:T(8,128)(2,1)}, bf16[2,1024,512]{2,1,0:T(8,128)(2,1)S(1)}, u32[]{:S(2)}, u32[]{:S(2)}) collective-permute-start(bf16[2,1024,512]{2,1,0:T(8,128)(2,1)} %get-tuple-element.831), channel_id=1, source_target_pairs={{0,8},{8,16},{16,24},{24,32},{32,40},{40,48},{48,56},{56,64},{64,7... | collective-permute-start | bytes 6291464 | tf_op jit(solution)/shard_map/while/body/eval_jaxpr/ppermute | solution.py:14
  733.1 5.1 copy-start.3
  796.1 29.3 %collective-permute-start = (bf16[2,1024,512]{2,1,0:T(8,128)(2,1)}, bf16[2,1024,512]{2,1,0:T(8,128)(2,1)S(1)}, u32[]{:S(2)}, u32[]{:S(2)}) collective-permute-start(bf16[2,1024,512]{2,1,0:T(8,128)(2,1)} %get-tuple-element.831), channel_id=1, source_target_pairs={{0,8},{8,16},{16,24},{24,32},{32,40},{40,48},{48,56},{56,64},{64,7... | collective-permute-start | bytes 6291464 | tf_op jit(solution)/shard_map/while/body/eval_jaxpr/ppermute | solution.py:14
  797.4 5.1 copy-start.3
  860.4 29.3 %collective-permute-start = (bf16[2,1024,512]{2,1,0:T(8,128)(2,1)}, bf16[2,1024,512]{2,1,0:T(8,128)(2,1)S(1)}, u32[]{:S(2)}, u32[]{:S(2)}) collective-permute-start(bf16[2,1024,512]{2,1,0:T(8,128)(2,1)} %get-tuple-element.831), channel_id=1, source_target_pairs={{0,8},{8,16},{16,24},{24,32},{32,40},{40,48},{48,56},{56,64},{64,7... | collective-permute-start | bytes 6291464 | tf_op jit(solution)/shard_map/while/body/eval_jaxpr/ppermute | solution.py:14
  861.7 5.1 copy-start.3
  924.6 29.3 %collective-permute-start = (bf16[2,1024,512]{2,1,0:T(8,128)(2,1)}, bf16[2,1024,512]{2,1,0:T(8,128)(2,1)S(1)}, u32[]{:S(2)}, u32[]{:S(2)}) collective-permute-start(bf16[2,1024,512]{2,1,0:T(8,128)(2,1)} %get-tuple-element.831), channel_id=1, source_target_pairs={{0,8},{8,16},{16,24},{24,32},{32,40},{40,48},{48,56},{56,64},{64,7... | collective-permute-start | bytes 6291464 | tf_op jit(solution)/shard_map/while/body/eval_jaxpr/ppermute | solution.py:14
  925.9 5.1 copy-start.3
  988.9 29.3 %collective-permute-start = (bf16[2,1024,512]{2,1,0:T(8,128)(2,1)}, bf16[2,1024,512]{2,1,0:T(8,128)(2,1)S(1)}, u32[]{:S(2)}, u32[]{:S(2)}) collective-permute-start(bf16[2,1024,512]{2,1,0:T(8,128)(2,1)} %get-tuple-element.831), channel_id=1, source_target_pairs={{0,8},{8,16},{16,24},{24,32},{32,40},{40,48},{48,56},{56,64},{64,7... | collective-permute-start | bytes 6291464 | tf_op jit(solution)/shard_map/while/body/eval_jaxpr/ppermute | solution.py:14
  990.2 5.1 copy-start.3
  1053.2 5.3 copy-start.4
  (258 other events, 652.3 us)
Sparse Core Ops, SparseCore 0:
  10.2 53.5 all-gather.1
where the time goes:
time: 1080 us; the launch traced here: 1070 us
  local copies, waits for them, and re-layouts  387 us (36%)
  waiting for transfers between devices  347 us (32%)
  other arithmetic  160 us (15%)
  matrix products  153 us (14%)
  between operations  15.5 us (1%)
    ppermute x15, waiting for transfers between devices, shifted(): lax.ppermute(array, axis, [(i, (i + by) % devices) for i in range(devices)])  303 us
    while x615, local copies, waits for them, and re-layouts  126 us
    dot_general x32, matrix products, attend(): jnp.einsum('rhgd,khd->rhgk', query_head_rows, key_head_rows, preferred_el...  90.3 us
    dot_general x32, matrix products, attend(): jnp.einsum('rhgk,khd->rhgd', attention_weights.astype(jnp.bfloat16), valu...  62.9 us
    reshape x16, local copies, waits for them, and re-layouts, attend(): updated_totals.reshape(count_of_rows, -1)  46.9 us
    convert_element_type x15, other arithmetic, attend(): attention_weights.astype(jnp.bfloat16)  46.7 us
    all_gather x1, waiting for transfers between devices, local(): group_pair = lax.all_gather(local_pair, 'inner', axis=1, tiled=True)  43.5 us
    reduce_sum x17, other arithmetic, attend(): jnp.sum(attention_weights, axis=3)  38 us
  transfers between devices with their start and end apart: 16, of which 16 were waited for; matrix products, arithmetic and copies ran while one was open for 14% of the time, Pallas kernels for 0%

commit v1 on v0

v1 whole, which is shorter than its diff:
```python
import math

import jax
import jax.numpy as jnp
from jax import lax
from jax.experimental import pallas as pl
from jax.experimental.pallas import tpu as pltpu
from jax.sharding import PartitionSpec as P

MESH = pl.DeviceIdType.MESH
HEADS = 4
GROUP = 8
HEAD = 128
HALF = 64
COLS = GROUP * HALF
UNIT = 16
KEYS = UNIT * HALF
PLANE = 64
SCALE = math.log2(math.e) / math.sqrt(HEAD)
NEG = -1e30
INIT, FIRST = 4, 5
OFFS = (0, 3, 1, 2)


def coords():
    o, i = lax.axis_index("outer"), lax.axis_index("inner")
    return o % 2, (o // 8) * 2 + i % 2, (o // 2) % 4, i // 2


def device(c, y, z, x):
    return ((y // 2 * 4 + z) * 2 + c, x * 2 + y % 2)


def slot_of(c, y, z, x):
    return ((c * 4 + y) * 4 + z) * 4 + x


def kernel(
    inv, bp, q_ref, k_ref, v_ref, o_ref, ck_ref, cv_ref,
    kv, so, qb, q2, osend, oland, csend, cland, ms, ls, acc, sa, sb, xa, xb,
    xs, xr, qs, qr, ps, pr, ss, sr, os_, or_, cs, cr,
):
    c, y, z, x = coords()
    me = device(c, y, z, x)

    def remote(src, dst, s, r, p):
        return pltpu.make_async_remote_copy(
            src_ref=src, dst_ref=dst, send_sem=s, recv_sem=r, device_id=p, device_id_type=MESH
        )

    def at(pos, n=2):
        return kv.at[pl.ds(pos, n)]

    def cols(h, w):
        return pl.ds(pl.multiple_of(h * w, w), w)

    peers = [device(c, y, z, (x + s) % 4) for s in (1, 2, 3)]
    peers += [device(c, (y + d) % 4, z, x) for d in (1, 3)]
    peers += [device(c, y, (z + d) % 4, x) for d in (1, 3)]
    peers += [device(1 - c, y, z, x)]
    bar = pltpu.get_barrier_semaphore()
    for p in peers:
        pl.semaphore_signal(bar, inc=1, device_id=p, device_id_type=MESH)
    pl.semaphore_wait(bar, len(peers))

    home = slot_of(c, y, z, x)

    def head_kv(s, a):
        h = (x + s) % 4
        ref = (k_ref, v_ref)[a]
        return remote(ref.at[:, cols(h, HEAD)], kv.at[home, a], xs.at[s - 1, a], xr.at[s - 1, a], device(c, y, z, h))

    def head_q(s):
        h = (x + s) % 4
        return remote(
            q_ref.at[:, cols(h, GROUP * HEAD)], qb.at[s - 1], qs.at[s - 1], qr.at[s - 1], device(c, y, z, h)
        )

    for s in (1, 3, 2):
        for a in (0, 1):
            head_kv(s, a).start()
    for s in (1, 3, 2):
        head_q(s).start()
    kv[home, 0] = k_ref[:, cols(x, HEAD)]
    kv[home, 1] = v_ref[:, cols(x, HEAD)]

    def pos(hf, df, dg):
        yy, zz = ((y + df) % 4, (z + dg) % 4) if hf == 0 else ((y + dg) % 4, (z + df) % 4)
        return slot_of(c, yy, zz, 2 * hf)

    def neighbour(hf, axis, d):
        if (axis == 0) == (hf == 0):
            return device(c, (y + d) % 4, z, x)
        return device(c, y, (z + d) % 4, x)

    def sem(hf, k, j):
        return hf * 20 + k * 4 + j

    def ring(hf, k, j):
        axis, df = (1, OFFS[k]) if k < 4 else (0, 0)
        n = sem(hf, k, j)
        if j < 2:
            src = at(pos(hf, df, 0))
            return remote(src, src, ps.at[n], pr.at[n], neighbour(hf, axis, (1, 3)[j]))
        e = OFFS[j - 1]
        where = pos(hf, df, e) if axis else pos(hf, e, 0)
        src = at(where + (j - 2), 1)
        return remote(src, src, ps.at[n], pr.at[n], neighbour(hf, axis, (1, 3)[j - 2]))

    def ring_in(hf, k, j):
        axis, df = (1, OFFS[k]) if k < 4 else (0, 0)
        n = sem(hf, k, j)
        e = OFFS[j + 1] if j < 2 else 2
        where = pos(hf, df, e) if axis else pos(hf, e, 0)
        ref = at(where) if j < 2 else at(where + (j - 2), 1)
        return remote(ref, ref, ps.at[n], pr.at[n], me)

    def sib_index(hf, df, dg):
        return (hf * 4 + df) * 4 + dg

    def sib(hf, df, dg, inward=False):
        n = sib_index(hf, df, dg)
        ref = at(pos(hf, df, dg) + ((1 - 2 * c) * PLANE if inward else 0))
        return remote(ref, ref, ss.at[n], sr.at[n], device(1 - c, y, z, x))

    def ring_send(hf, k):
        for j in (0, 1):
            ring(hf, k, j).start()

    def ring_recv(hf, k, j):
        ring_in(hf, k, j).wait_recv()
        ring(hf, k, 2 + j).start()
        e = OFFS[1 + j]
        sib(hf, *((e, 0) if k == 4 else (OFFS[k], e))).start()

    def ring_far(hf, k):
        for j in (2, 3):
            ring_in(hf, k, j).wait_recv()
        sib(hf, *((2, 0) if k == 4 else (OFFS[k], 2))).start()

    for s in (1, 3, 2):
        src = slot_of(c, y, z, (x + 4 - s) % 4)
        for a in (0, 1):
            ref = kv.at[src, a]
            remote(ref, ref, xs.at[s - 1, a], xr.at[s - 1, a], me).wait_recv()
    for hf in (0, 1):
        ring_send(hf, 4)
    for hf in (0, 1):
        ring_send(hf, 0)
        sib(hf, 0, 0).start()

    for g in range(GROUP):
        w = q_ref[:, pl.ds(pl.multiple_of(x * (GROUP * HEAD) + g * HEAD, HEAD), HEAD)]
        for e in (0, 1):
            q2[0, e, g * HALF : (g + 1) * HALF, :] = w[e * HALF : (e + 1) * HALF]
    ms[...] = jnp.full_like(ms, NEG)
    ls[...] = jnp.zeros_like(ls)
    acc[0:FIRST] = jnp.zeros((FIRST, HEAD, COLS), jnp.float32)

    bufs, tops = (sa, sb), (xa, xb)

    def scores(b, keys, queries, mask=None):
        s = lax.dot_general(keys, queries, (((1,), (1,)), ((), ())), preferred_element_type=jnp.float32)
        if mask is not None:
            s = jnp.where(mask, s, NEG)
        bufs[b][...] = s
        tops[b][...] = jnp.max(s.reshape(KEYS // 8, 8, COLS), axis=0)

    def accumulate(b, values, prev, to):
        old = ms[prev]
        new = jnp.maximum(old, jnp.max(tops[b][...], axis=0, keepdims=True) * SCALE)
        fade = jnp.exp2(old - new)
        p = jnp.exp2(bufs[b][...] * SCALE - new)
        ms[to] = new
        ls[to] = ls[prev] * fade + jnp.sum(p.reshape(KEYS // 8, 8, COLS), axis=0)
        add = lax.dot_general(
            values, p.astype(jnp.bfloat16), (((0,), (0,)), ((), ())), preferred_element_type=jnp.float32
        )
        acc[to] = acc[prev] * fade + add

    def sib_wait(dy):
        for e in range(4):
            sib(0, dy, e, True).wait_recv()
            sib(1, e, dy, True).wait_recv()

    def step0():
        for k in (1, 2):
            for hf in (0, 1):
                ring_recv(hf, 4, k - 1)
                ring_send(hf, k)
        for hf in (0, 1):
            ring_far(hf, 4)
            ring_send(hf, 3)
        for j in (0, 1):
            for hf in (0, 1):
                ring_recv(hf, 0, j)
        for s in (1, 3, 2):
            remote(qb.at[s - 1], qb.at[s - 1], qs.at[s - 1], qr.at[s - 1], me).wait_recv()
            for g in range(GROUP):
                w = qb[s - 1, :, g * HEAD : (g + 1) * HEAD]
                for e in (0, 1):
                    q2[s, e, g * HALF : (g + 1) * HALF, :] = w[e * HALF : (e + 1) * HALF]
        for j in (0, 1):
            for hf in (0, 1):
                ring_recv(hf, 1, j)
        ring_far(0, 0)

    def step1():
        for j in (0, 1):
            for hf in (0, 1):
                ring_recv(hf, 2, j)
        sib_wait(0)

    def step2():
        for j in (0, 1):
            for hf in (0, 1):
                ring_recv(hf, 3, j)
        ring_far(0, 1)

    def step3():
        ring_far(1, 0)
        sib_wait(3)

    def step4():
        ring_far(0, 2)
        ring_far(1, 1)

    def step5():
        ring_far(0, 3)
        ring_far(1, 2)
        sib_wait(1)

    def step6():
        ring_far(1, 3)

    def step7():
        sib_wait(2)

    def dense(i, _):
        for n, step in enumerate((step0, step1, step2, step3, step4, step5, step6, step7)):
            pl.when(i == n)(step)
        turn = i // 2
        dy = (3 * turn + 3 * (turn // 2) + 2 * (turn // 3)) % 4
        base = slot_of((c + i) % 2, (y + dy) % 4, 0, 0)
        keys = kv[pl.ds(base, UNIT), 0, 0:HALF, :].reshape(KEYS, HEAD)
        values = kv[pl.ds(base, UNIT), 1, 0:HALF, :].reshape(KEYS, HEAD)
        scores(0, keys, q2[0, 1])
        for s in range(4):
            if s < 3:
                scores((s + 1) % 2, keys, q2[s + 1, 1])
            accumulate(s % 2, values, s, s)
        return 0

    lax.fori_loop(0, 8, dense, 0)

    def order(t, _):
        src = inv[0, t]
        so[0, t] = kv[src, 0, 0:HALF, :]
        so[1, t] = kv[src, 0, HALF : 2 * HALF, :]
        so[2, t] = kv[src, 1, 0:HALF, :]
        so[3, t] = kv[src, 1, HALF : 2 * HALF, :]
        return 0

    lax.fori_loop(0, 128, order, 0, unroll=4)

    def cache_out(s):
        return remote(csend.at[s], cland.at[x], cs.at[s - 1], cr.at[s - 1], device(c, y, z, (x + 4 - s) % 4))

    for s in (1, 3, 2, 0):
        po, pi = device(c, y, z, (x + 4 - s) % 4)
        for e in (0, 1):
            code = inv[1, (po * 8 + pi) * 2 + e]
            at_b, which = lax.div(code, 2), lax.rem(code, 2)
            for a in (0, 1):
                piece = so[2 * a + which, at_b]
                if s:
                    csend[s, a, e * HALF : (e + 1) * HALF, :] = piece
                else:
                    cland[x, a, e * HALF : (e + 1) * HALF, :] = piece
        if s:
            cache_out(s).start()

    key_at = lax.broadcasted_iota(jnp.int32, (KEYS, COLS), 0)
    row_at = lax.broadcasted_iota(jnp.int32, (KEYS, COLS), 1) % HALF

    def out_copy(s):
        return remote(osend.at[s], oland.at[x], os_.at[s - 1], or_.at[s - 1], device(c, y, z, (x + 4 - s) % 4))

    def block(n, _):
        s = (n + 1) % 4
        po, pi = device(c, y, z, (x + 4 - s) % 4)
        b = bp[(po * 8 + pi) * 2]
        full = lax.div(b, UNIT)
        left = b - full * UNIT
        units = []
        for u in range(7):
            late = lax.div(u - full + 8, 8)
            other = lax.div((u - full) * (u - full) + 48, 49)
            prev = s + other * (INIT + u - s)
            units.append((late, u + late, prev, FIRST + u, None))
        early_mask = key_at <= left * HALF + row_at
        late_mask = (left - key_at // HALF) * HALF + key_at % HALF <= row_at
        units.append((0, full, INIT + full, FIRST + 7, early_mask))
        units.append((1, full, FIRST + 6 + lax.div(full, 7) * (s - FIRST - 6), FIRST + 8, late_mask))

        def first(m):
            late, ch, _, _, mask = units[m]
            scores(m % 2, so[late, pl.ds(ch * UNIT, UNIT)].reshape(KEYS, HEAD), q2[s, late], mask)

        first(0)
        for m in range(9):
            if m < 8:
                first(m + 1)
            late, ch, prev, to, _ = units[m]
            accumulate(m % 2, so[2 + late, pl.ds(ch * UNIT, UNIT)].reshape(KEYS, HEAD), prev, to)
        for e in (0, 1):
            total = jnp.sum(ls[FIRST + 7 + e], axis=0, keepdims=True)
            res = (acc[FIRST + 7 + e] / total).T.astype(jnp.bfloat16)
            for g in range(GROUP):
                osend[s, e * HALF : (e + 1) * HALF, g * HEAD : (g + 1) * HEAD] = res[g * HALF : (g + 1) * HALF]
        pl.when(n < 3)(lambda: out_copy(s).start())
        return 0

    lax.fori_loop(0, 4, block, 0)

    for s in (1, 3, 2):
        h = (x + s) % 4
        remote(csend.at[s], cland.at[h], cs.at[s - 1], cr.at[s - 1], me).wait_recv()
        remote(osend.at[s], oland.at[h], os_.at[s - 1], or_.at[s - 1], me).wait_recv()
    o_ref[:, cols(x, GROUP * HEAD)] = osend[0]
    for s in (1, 3, 2):
        h = (x + s) % 4
        o_ref[:, cols(h, GROUP * HEAD)] = oland[h]
    for h in range(HEADS):
        ck_ref[:, h * HEAD : (h + 1) * HEAD] = cland[h, 0]
        cv_ref[:, h * HEAD : (h + 1) * HEAD] = cland[h, 1]

    for s in (1, 2, 3):
        for a in (0, 1):
            head_kv(s, a).wait_send()
        head_q(s).wait_send()
        cache_out(s).wait_send()
        out_copy(s).wait_send()
    for hf in (0, 1):
        for k in range(5):
            for j in range(4):
                ring(hf, k, j).wait_send()
        for df in range(4):
            for dg in range(4):
                sib(hf, df, dg).wait_send()


def local(queries, keys, values, block_pos, cache_slot):
    rows, width = queries.shape
    j = jnp.arange(256, dtype=jnp.int32)
    d = j // 2
    o, i = d // 8, d % 8
    slot = slot_of(o % 2, o // 8 * 2 + i % 2, o // 2 % 4, i // 2)
    place = jnp.repeat(block_pos[::2], 2) * 2 + j % 2
    both = jnp.stack([block_pos, cache_slot])
    what = jnp.stack([slot, place])
    inv = jnp.sum(jnp.where(both[:, None, :] == j[None, :, None], what[:, None, :], 0), axis=2)
    bf, f32 = jnp.bfloat16, jnp.float32
    dma = pltpu.SemaphoreType.DMA
    vmem = pl.BlockSpec(memory_space=pltpu.VMEM)
    smem = pl.BlockSpec(memory_space=pltpu.SMEM)
    return pl.pallas_call(
        kernel,
        out_shape=(
            jax.ShapeDtypeStruct((rows, width), bf),
            jax.ShapeDtypeStruct(keys.shape, bf),
            jax.ShapeDtypeStruct(values.shape, bf),
        ),
        in_specs=[smem, smem, vmem, vmem, vmem],
        out_specs=(vmem, vmem, vmem),
        scratch_shapes=[
            pltpu.VMEM((128, 2, 2 * HALF, HEAD), bf),
            pltpu.VMEM((4, 128, HALF, HEAD), bf),
            pltpu.VMEM((3, rows, GROUP * HEAD), bf),
            pltpu.VMEM((4, 2, COLS, HEAD), bf),
            pltpu.VMEM((4, rows, GROUP * HEAD), bf),
            pltpu.VMEM((4, rows, GROUP * HEAD), bf),
            pltpu.VMEM((4, 2, rows, HEAD), bf),
            pltpu.VMEM((4, 2, rows, HEAD), bf),
            pltpu.VMEM((FIRST + 9, 1, COLS), f32),
            pltpu.VMEM((FIRST + 9, 8, COLS), f32),
            pltpu.VMEM((FIRST + 9, HEAD, COLS), f32),
            pltpu.VMEM((KEYS, COLS), f32),
            pltpu.VMEM((KEYS, COLS), f32),
            pltpu.VMEM((8, COLS), f32),
            pltpu.VMEM((8, COLS), f32),
            dma((3, 2)), dma((3, 2)), dma((3,)), dma((3,)),
            dma((40,)), dma((40,)), dma((32,)), dma((32,)),
            dma((3,)), dma((3,)), dma((3,)), dma((3,)),
        ],
        compiler_params=pltpu.CompilerParams(
            collective_id=0, has_side_effects=True, vmem_limit_bytes=56 * 1024 * 1024
        ),
    )(inv, block_pos, queries, keys, values)


def solution(mesh):
    rows = P(("outer", "inner"), None)
    return jax.shard_map(
        local,
        mesh=mesh,
        in_specs=(rows, rows, rows, P(), P()),
        out_specs=(rows, rows, rows),
        check_vma=False,
    )
```

time: 1080 us -> 91.9 us (0.09); the launches traced: 1070 us -> 91.7 us
  local copies, waits for them, and re-layouts: 387 us -> 5.71 us
  waiting for transfers between devices: 347 us -> 0 us
  other arithmetic: 160 us -> 0.79 us
  matrix products: 153 us -> 0 us
  Pallas kernels: 0 us -> 84.5 us
  between operations: 15.5 us -> 0.69 us
    ppermute x15 -> x0, waiting for transfers between devices: 303 us -> none  [shifted(): lax.ppermute(array, axis, [(i, (i + by) % devices) for i in range(devices)])]
    dot_general x64 -> x0, matrix products: 153 us -> none  [the longest x32 90.3 us: attend(): jnp.einsum('rhgd,khd->rhgk', query_head_rows, key_head_rows, preferred_el...]
    while x617 -> x0, local copies, waits for them, and re-layouts: 128 us -> none
    slice x83 -> x1, local copies, waits for them, and re-layouts: 120 us -> 0.22 us  [local(): place = jnp.repeat(block_pos[::2], 2) * 2 + j % 2]
    pallas_call x0 -> x1, Pallas kernels: none -> 84.5 us  [local(): pl.pallas_call(kernel, out_shape=(jax.ShapeDtypeStruct((rows, width), bf)...]
    squeeze x30 -> x0, local copies, waits for them, and re-layouts: 59.3 us -> none  [the longest x15 29.9 us: attend(): value_row_block.reshape(-1, LOCAL_KEY_HEADS, HEAD_DIMENSION)]
    reduce_sum x35 -> x1, other arithmetic: 56.3 us -> 0.73 us  [local(): jnp.sum(jnp.where(both[:, None, :] == j[None, :, None], what[:, None, :],...]
    convert_element_type x17 -> x0, other arithmetic: 48.2 us -> none  [the longest x15 46.7 us: attend(): attention_weights.astype(jnp.bfloat16)]
  transfers between devices with their start and end apart: 16 -> 0, of which waited for: 16 -> 0; matrix products, arithmetic and copies ran while one was open for 14% -> 0% of each run, Pallas kernels for 0% -> 0%
where the time goes in v1:
time: 91.9 us; the launch traced here: 91.7 us
  Pallas kernels  84.5 us (92%)
  local copies, waits for them, and re-layouts  5.71 us (6%)
    pallas_call x1, Pallas kernels, local(): pl.pallas_call(kernel, out_shape=(jax.ShapeDtypeStruct((rows, width), bf)...  84.5 us
    unnamed x11, local copies, waits for them, and re-layouts  5.27 us

profile of v1, /device:TPU:0, one launch (start us, length us, event | category | flops | bytes accessed | tf_op | source)
XLA Modules:
  0.0 91.7 jit_solution(10129543755227308934)
XLA Ops:
  0.6 0.0 copy-start.2
  0.6 0.7 copy-done.2
  1.3 0.2 slice.3
  1.5 0.0 copy-start.3
  1.6 0.7 copy-done.3
  2.2 0.1 broadcast_in_dim.18
  2.3 0.1 mul.59
  2.5 0.7 select_reduce_fusion.inv
  3.2 84.5 %shard_map.76 = (bf16[128,4096]{1,0:T(8,128)(2,1)}, bf16[128,512]{1,0:T(8,128)(2,1)}, bf16[128,512]{1,0:T(8,128)(2,1)}) custom-call(s32[2,256]{1,0:T(2,128)} %select_reduce_fusion.inv, s32[256]{0:T(256)} %bp.1, bf16[128,4096]{1,0:T(8,128)(2,1)} %q_ref.1, bf16[128,512]{1,0:T(8,128)(2,1)} %k_ref.1, bf16[128,512]{1,0:T(8,128)(2,1)} %v_ref.1), custom_call_target="tpu_custom_call" | custom-call | tf_op jit(solution)/shard_map/pallas_call | solution.py:367
  87.8 0.0 copy-start.1
  87.8 2.3 %copy.11 = bf16[128,4096]{1,0:T(8,128)(2,1)} copy(bf16[128,4096]{1,0:T(8,128)(2,1)} %get-tuple-element.8) | data formatting | bytes 2097152
  90.1 0.0 copy-done.1
  90.1 0.0 copy-start
  90.1 0.7 copy.12
  90.8 0.3 copy-done
  91.0 0.7 copy.13
  (4 shorter events, 0.1 us)
Async XLA Ops:
  0.6 0.7 copy-start.2
  1.5 0.7 copy-start.3
  87.8 2.3 %copy-start.1 = (bf16[128,512]{1,0:T(8,128)(2,1)S(1)}, bf16[128,512]{1,0:T(8,128)(2,1)}, u32[]{:S(2)}) copy-start(bf16[128,512]{1,0:T(8,128)(2,1)} %get-tuple-element.9) | copy-start | bytes 393220
  90.1 1.0 %copy-start = (bf16[128,512]{1,0:T(8,128)(2,1)S(1)}, bf16[128,512]{1,0:T(8,128)(2,1)}, u32[]{:S(2)}) copy-start(bf16[128,512]{1,0:T(8,128)(2,1)} %get-tuple-element.10) | copy-start | bytes 393220

commit v2 on v1

v2 whole, which is shorter than its diff:
```python
import math

import jax
import jax.numpy as jnp
from jax import lax
from jax.experimental import pallas as pl
from jax.experimental.pallas import tpu as pltpu
from jax.sharding import PartitionSpec as P

MESH = pl.DeviceIdType.MESH
HEADS = 4
GROUP = 8
HEAD = 128
HALF = 64
COLS = GROUP * HALF
UNIT = 16
KEYS = UNIT * HALF
PLANE = 64
SCALE = math.log2(math.e) / math.sqrt(HEAD)
NEG = -1e30
OFFS = (0, 3, 1, 2)


def coords():
    o, i = lax.axis_index("outer"), lax.axis_index("inner")
    return o % 2, (o // 8) * 2 + i % 2, (o // 2) % 4, i // 2


def device(c, y, z, x):
    return ((y // 2 * 4 + z) * 2 + c, x * 2 + y % 2)


def slot_of(c, y, z, x):
    return ((c * 4 + y) * 4 + z) * 4 + x


def kernel(
    inv, bp, q_hbm, k_hbm, v_hbm, o_ref, ck_ref, cv_ref,
    q_ref, k_ref, v_ref, kv, qb, q2, osend, oland, csend, cland, ms, mb, ls, acc, sa, sb, xa, xb,
    ld, xs, xr, qs, qr, ps, pr, ss, sr, os_, or_, cs, cr,
):
    c, y, z, x = coords()
    me = device(c, y, z, x)
    loads = [
        pltpu.make_async_copy(src, dst, ld.at[n])
        for n, (src, dst) in enumerate(((k_hbm, k_ref), (v_hbm, v_ref), (q_hbm, q_ref)))
    ]
    for load in loads:
        load.start()

    def remote(src, dst, s, r, p):
        return pltpu.make_async_remote_copy(
            src_ref=src, dst_ref=dst, send_sem=s, recv_sem=r, device_id=p, device_id_type=MESH
        )

    def at(pos, n=2):
        return kv.at[pl.ds(pos, n)]

    def cols(h, w):
        return pl.ds(pl.multiple_of(h * w, w), w)

    peers = [device(c, y, z, (x + s) % 4) for s in (1, 2, 3)]
    peers += [device(c, (y + d) % 4, z, x) for d in (1, 2, 3)]
    peers += [device(c, y, (z + d) % 4, x) for d in (1, 2, 3)]
    peers += [device(1 - c, y, z, x)]
    bar = pltpu.get_barrier_semaphore()
    for p in peers:
        pl.semaphore_signal(bar, inc=1, device_id=p, device_id_type=MESH)
    pl.semaphore_wait(bar, len(peers))
    for load in loads:
        load.wait()

    home = slot_of(c, y, z, x)

    def head_kv(s, a):
        h = (x + s) % 4
        ref = (k_ref, v_ref)[a]
        return remote(ref.at[:, :, cols(h, HEAD)], kv.at[home, a], xs.at[s - 1, a], xr.at[s - 1, a], device(c, y, z, h))

    def head_q(s):
        h = (x + s) % 4
        return remote(
            q_ref.at[:, :, cols(h, GROUP * HEAD)], qb.at[s - 1], qs.at[s - 1], qr.at[s - 1], device(c, y, z, h)
        )

    for s in (1, 3, 2):
        for a in (0, 1):
            head_kv(s, a).start()
    for s in (1, 3, 2):
        head_q(s).start()
    kv[home, 0] = k_ref[:, :, cols(x, HEAD)]
    kv[home, 1] = v_ref[:, :, cols(x, HEAD)]

    def pos(hf, df, dg):
        yy, zz = ((y + df) % 4, (z + dg) % 4) if hf == 0 else ((y + dg) % 4, (z + df) % 4)
        return slot_of(c, yy, zz, 2 * hf)

    def neighbour(hf, axis, d):
        if (axis == 0) == (hf == 0):
            return device(c, (y + d) % 4, z, x)
        return device(c, y, (z + d) % 4, x)

    def sem(hf, k, j):
        return hf * 20 + k * 4 + j

    def ring(hf, k, j):
        axis, df = (1, OFFS[k]) if k < 4 else (0, 0)
        src, n = at(pos(hf, df, 0)), sem(hf, k, j)
        return remote(src, src, ps.at[n], pr.at[n], neighbour(hf, axis, (1, 3, 2)[j]))

    def ring_in(hf, k, j):
        e, n = OFFS[j + 1], sem(hf, k, j)
        at_f, at_g = (OFFS[k], e) if k < 4 else (e, 0)
        ref = at(pos(hf, at_f, at_g))
        remote(ref, ref, ps.at[n], pr.at[n], me).wait_recv()
        sib(hf, at_f, at_g).start()

    def sib_index(hf, df, dg):
        return (hf * 4 + df) * 4 + dg

    def sib(hf, df, dg, inward=False):
        n = sib_index(hf, df, dg)
        ref = at(pos(hf, df, dg) + ((1 - 2 * c) * PLANE if inward else 0))
        return remote(ref, ref, ss.at[n], sr.at[n], device(1 - c, y, z, x))

    def ring_send(k, copies=(0, 1, 2)):
        for hf in (0, 1):
            for j in copies:
                ring(hf, k, j).start()

    def ring_wait(k, copies=(0, 1, 2)):
        for hf in (0, 1):
            for j in copies:
                ring_in(hf, k, j)

    for s in (1, 3, 2):
        src = slot_of(c, y, z, (x + 4 - s) % 4)
        for a in (0, 1):
            ref = kv.at[src, a]
            remote(ref, ref, xs.at[s - 1, a], xr.at[s - 1, a], me).wait_recv()
    ring_send(4, (0, 1))
    ring_send(0)
    for hf in (0, 1):
        sib(hf, 0, 0).start()

    def regroup(s, get):
        for g in range(GROUP):
            w = get(g)
            for e in (0, 1):
                q2[s, g * HALF : (g + 1) * HALF, e * HEAD : (e + 1) * HEAD] = w[e]

    regroup(0, lambda g: q_ref[:, :, pl.ds(pl.multiple_of(x * (GROUP * HEAD) + g * HEAD, HEAD), HEAD)])

    def sib_wait(k):
        for hf in (0, 1):
            for e in range(4):
                sib(hf, OFFS[k], e, True).wait_recv()

    ring_wait(4, (0, 1))
    ring_send(1)
    ring_send(4, (2,))
    for s in (1, 3, 2):
        remote(qb.at[s - 1], qb.at[s - 1], qs.at[s - 1], qr.at[s - 1], me).wait_recv()
        regroup(s, lambda g: qb[s - 1, :, :, g * HEAD : (g + 1) * HEAD])

    def owner(s):
        po, pi = device(c, y, z, (x + 4 - s) % 4)
        return po * 8 + pi

    def dot_scores(keys, queries):
        return lax.dot_general(keys, queries, (((1,), (1,)), ((), ())), preferred_element_type=jnp.float32)

    def dot_values(values, p):
        return lax.dot_general(
            values, p.astype(jnp.bfloat16), (((0,), (0,)), ((), ())), preferred_element_type=jnp.float32
        )

    def diagonal(s, _):
        src = slot_of(c, y, z, (x + 4 - s) % 4)
        shape = (HALF, COLS)
        seen = lax.broadcasted_iota(jnp.int32, shape, 0) <= lax.broadcasted_iota(jnp.int32, shape, 1) % HALF
        for e in (0, 1):
            t = jnp.where(seen, dot_scores(kv[src, 0, e], q2[s, :, e * HEAD : (e + 1) * HEAD]) * SCALE, NEG)
            top = jnp.max(t, axis=0, keepdims=True)
            p = jnp.exp2(t - top)
            ms[s, e] = top
            ls[s, e] = jnp.sum(p.reshape(HALF // 8, 8, COLS), axis=0)
            acc[s, e] = dot_values(kv[src, 1, e], p)
        return 0

    lax.fori_loop(0, 4, diagonal, 0)
    ring_wait(0)

    bufs, tops = (sa, sb), (xa, xb)

    def chunk(i):
        turn = i // 2
        d = (3 * turn + 3 * (turn // 2) + 2 * (turn // 3)) % 4
        cc, yy, zz = (c + i) % 2, (y + d) % 4, (z + d) % 4
        bases, places = [], []
        for n in range(8):
            ys, zs, xs_ = (yy, n, 0) if n < 4 else (n - 4, zz, 2)
            bases.append(slot_of(cc, ys, zs, xs_))
            for t in (0, 1):
                po, pi = device(cc, ys, zs, xs_ + t)
                places.append(bp[(po * 8 + pi) * 2])
        return bases, places

    def sides(places, s):
        b = bp[owner(s) * 2]
        early, itself = [], []
        for place in places:
            d = b - place
            early.append(lax.div(d + 127, 128).astype(jnp.float32))
            itself.append((1 - lax.div(d * d + 16383, 16384)).astype(jnp.float32))
        return early, itself

    def put_scores(n, s):
        bufs[n][...] = s
        tops[n][...] = jnp.max(s.reshape(UNIT, HALF // 8, 8, COLS), axis=1)

    def pick(base, a, early):
        rows = []
        for t, e in enumerate(early):
            w = jnp.broadcast_to(jnp.full((16, HEAD), e, jnp.float32).astype(jnp.bfloat16)[None], (4, 16, HEAD)).reshape(HALF, HEAD)
            at_t = base[t // 2] + t % 2
            rows.append(jnp.concatenate([kv[at_t, a, 0] * w, kv[at_t, a, 1] * (1 - w)], axis=1))
        return jnp.concatenate(rows, axis=0)

    def early_rows(base, a):
        return jnp.concatenate([kv[pl.ds(b, 2), a, 0].reshape(2 * HALF, HEAD) for b in base], axis=0)

    def dense_scores(n, base, s):
        put_scores(n, dot_scores(early_rows(base, 0), q2[s, :, HEAD:]))

    def dense_sum(n, base, s):
        old = ms[s, 1]
        new = jnp.maximum(old, jnp.max(jnp.max(tops[n][...], axis=0), axis=0, keepdims=True) * SCALE)
        fade = jnp.exp2(old - new)
        ms[s, 1] = new
        p = jnp.exp2(bufs[n][...] * SCALE - ms[s, 1])
        ls[s, 1] = ls[s, 1] * fade + jnp.sum(p.reshape(KEYS // 8, 8, COLS), axis=0)
        acc[s, 1] = acc[s, 1] * fade + dot_values(early_rows(base, 1), p)

    def side_scores(n, base, s, side):
        put_scores(n, dot_scores(pick(base, 0, side[0]), q2[s]))

    def side_sum(n, base, s, side):
        early, itself = side
        new, fade = [], []
        for e in (0, 1):
            top = None
            for t in range(UNIT):
                off = (early[t] - 1.0) if e == 0 else (0.0 - early[t] - itself[t])
                w = tops[n][t] + off * -NEG
                top = w if top is None else jnp.maximum(top, w)
            old = ms[s, e]
            new.append(jnp.maximum(old, jnp.max(top, axis=0, keepdims=True) * SCALE))
            fade.append(jnp.exp2(old - new[e]))
            ms[s, e] = new[e]
        parts, sums = [], [ls[s, 0] * fade[0], ls[s, 1] * fade[1]]
        for t in range(UNIT):
            mb[n, t] = new[0] * early[t] + (new[1] * (1.0 - early[t]) + itself[t] * -NEG)
            p = jnp.exp2(bufs[n][t * HALF : (t + 1) * HALF] * SCALE - mb[n, t])
            w = jnp.sum(p.reshape(HALF // 8, 8, COLS), axis=0)
            sums[0] += w * early[t]
            sums[1] += w * (1.0 - early[t])
            parts.append(p.astype(jnp.bfloat16))
        add = dot_values(pick(base, 1, early), jnp.concatenate(parts, axis=0))
        for e in (0, 1):
            ls[s, e] = sums[e]
            acc[s, e] = acc[s, e] * fade[e] + add[e * HEAD : (e + 1) * HEAD]

    def run(units):
        for n, (first, _) in enumerate(units[:1]):
            first(n % 2)
        for n, (_, second) in enumerate(units):
            if n + 1 < len(units):
                units[n + 1][0]((n + 1) % 2)
            second(n % 2)

    def dense_unit(base, s):
        return (lambda n: dense_scores(n, base, s)), (lambda n: dense_sum(n, base, s))

    def side_unit(base, places, s):
        side = sides(places, s)
        return (lambda n: side_scores(n, base, s, side)), (lambda n: side_sum(n, base, s, side))

    def step1():
        ring_send(2)
        sib_wait(0)

    def step2():
        ring_wait(4, (2,))
        ring_send(3)
        ring_wait(1)

    def step3():
        sib_wait(1)

    def step4():
        ring_wait(2)

    def step5():
        sib_wait(2)
        ring_wait(3)

    def arriving(i, _):
        for n, step in enumerate((step1, step2, step3, step4, step5)):
            pl.when(i == n + 1)(step)
        base, places = chunk(i)
        units = []
        for s in (1, 2, 3):
            units += [dense_unit(base, s), side_unit(base, places, s)]
        run(units)
        return 0

    lax.fori_loop(0, 6, arriving, 0)
    sib_wait(3)

    def cache_out(s):
        return remote(csend.at[s], cland.at[x], cs.at[s - 1], cr.at[s - 1], device(c, y, z, (x + 4 - s) % 4))

    for s in (1, 3, 2, 0):
        for e in (0, 1):
            code = inv[owner(s) * 2 + e]
            for a in (0, 1):
                piece = kv[lax.div(code, 2), a, lax.rem(code, 2)]
                if s:
                    csend[s, a, e] = piece
                else:
                    cland[x, a, e] = piece
        if s:
            cache_out(s).start()

    def out_copy(s):
        return remote(osend.at[s], oland.at[x], os_.at[s - 1], or_.at[s - 1], device(c, y, z, (x + 4 - s) % 4))

    def last(n, _):
        own = (n + 4) // 7
        s = (n + 1) * (1 - own)
        pair = 3 * (1 - own) + (n - 3) * own
        both = [chunk(2 * pair), chunk(2 * pair + 1)]
        run([dense_unit(base, s) for base, _ in both] + [side_unit(base, places, s) for base, places in both])
        @pl.when(own == n // 6)
        def _():
            for e in (0, 1):
                total = jnp.sum(ls[s, e], axis=0, keepdims=True)
                res = (acc[s, e] / total).T.astype(jnp.bfloat16)
                for g in range(GROUP):
                    osend[s, e, :, g * HEAD : (g + 1) * HEAD] = res[g * HALF : (g + 1) * HALF]

        pl.when(n < 3)(lambda: out_copy(s).start())
        return 0

    lax.fori_loop(0, 7, last, 0)

    for s in (1, 3, 2):
        h = (x + s) % 4
        remote(csend.at[s], cland.at[h], cs.at[s - 1], cr.at[s - 1], me).wait_recv()
        remote(osend.at[s], oland.at[h], os_.at[s - 1], or_.at[s - 1], me).wait_recv()
    o_ref[:, :, cols(x, GROUP * HEAD)] = osend[0]
    for s in (1, 3, 2):
        h = (x + s) % 4
        o_ref[:, :, cols(h, GROUP * HEAD)] = oland[h]
    for h in range(HEADS):
        ck_ref[:, :, h * HEAD : (h + 1) * HEAD] = cland[h, 0]
        cv_ref[:, :, h * HEAD : (h + 1) * HEAD] = cland[h, 1]

    for s in (1, 2, 3):
        for a in (0, 1):
            head_kv(s, a).wait_send()
        head_q(s).wait_send()
        cache_out(s).wait_send()
        out_copy(s).wait_send()
    for hf in (0, 1):
        for k in range(5):
            for j in range(3):
                ring(hf, k, j).wait_send()
        for df in range(4):
            for dg in range(4):
                sib(hf, df, dg).wait_send()


def local(queries, keys, values, block_pos, cache_slot):
    j = jnp.arange(256, dtype=jnp.int32)
    d = j // 2
    o, i = d // 8, d % 8
    code = slot_of(o % 2, o // 8 * 2 + i % 2, o // 2 % 4, i // 2) * 2 + j % 2
    inv = jnp.sum(jnp.where(cache_slot[None, :] == j[:, None], code, 0), axis=1)
    bf, f32 = jnp.bfloat16, jnp.float32
    dma = pltpu.SemaphoreType.DMA
    vmem = pl.BlockSpec(memory_space=pltpu.VMEM)
    smem = pl.BlockSpec(memory_space=pltpu.SMEM)
    hbm = pl.BlockSpec(memory_space=pl.ANY)
    split = [a.reshape(2, HALF, a.shape[1]) for a in (queries, keys, values)]
    wide = (2, HALF, GROUP * HEAD)
    outs = pl.pallas_call(
        kernel,
        out_shape=tuple(jax.ShapeDtypeStruct(a.shape, bf) for a in split),
        in_specs=[smem, smem, hbm, hbm, hbm],
        out_specs=(vmem, vmem, vmem),
        scratch_shapes=[
            *(pltpu.VMEM(a.shape, bf) for a in split),
            pltpu.VMEM((128, 2, 2, HALF, HEAD), bf),
            pltpu.VMEM((3, *wide), bf),
            pltpu.VMEM((4, COLS, 2 * HEAD), bf),
            pltpu.VMEM((4, *wide), bf),
            pltpu.VMEM((4, *wide), bf),
            pltpu.VMEM((4, 2, 2, HALF, HEAD), bf),
            pltpu.VMEM((4, 2, 2, HALF, HEAD), bf),
            pltpu.VMEM((4, 2, 1, COLS), f32),
            pltpu.VMEM((2, UNIT, 1, COLS), f32),
            pltpu.VMEM((4, 2, 8, COLS), f32),
            pltpu.VMEM((4, 2, HEAD, COLS), f32),
            pltpu.VMEM((KEYS, COLS), f32),
            pltpu.VMEM((KEYS, COLS), f32),
            pltpu.VMEM((UNIT, 8, COLS), f32),
            pltpu.VMEM((UNIT, 8, COLS), f32),
            dma((3,)), dma((3, 2)), dma((3, 2)), dma((3,)), dma((3,)),
            dma((40,)), dma((40,)), dma((32,)), dma((32,)),
            dma((3,)), dma((3,)), dma((3,)), dma((3,)),
        ],
        compiler_params=pltpu.CompilerParams(
            collective_id=0, has_side_effects=True, vmem_limit_bytes=56 * 1024 * 1024
        ),
    )(inv, block_pos, *split)
    return tuple(o.reshape(a.shape) for o, a in zip(outs, (queries, keys, values)))


def solution(mesh):
    rows = P(("outer", "inner"), None)
    return jax.shard_map(
        local,
        mesh=mesh,
        in_specs=(rows, rows, rows, P(), P()),
        out_specs=(rows, rows, rows),
        check_vma=False,
    )
```

time: 91.9 us -> 85.4 us (0.929)
  Pallas kernels: 84.5 us -> 79.3 us
  local copies, waits for them, and re-layouts: 5.71 us -> 4.58 us
    pallas_call x1, Pallas kernels: 84.5 us -> 79.3 us  [local(): pl.pallas_call(kernel, out_shape=tuple((jax.ShapeDtypeStruct(a.shape, bf)...]
    unnamed x11 -> x9, local copies, waits for them, and re-layouts: 5.27 us -> 4.58 us
where the time goes in v2:
time: 85.4 us; the launch traced here: 85.2 us
  Pallas kernels  79.3 us (93%)
  local copies, waits for them, and re-layouts  4.58 us (5%)
    pallas_call x1, Pallas kernels, local(): pl.pallas_call(kernel, out_shape=tuple((jax.ShapeDtypeStruct(a.shape, bf)...  79.3 us
    unnamed x9, local copies, waits for them, and re-layouts  4.58 us

profile of v2, /device:TPU:0, one launch (start us, length us, event | category | flops | bytes accessed | tf_op | source)
XLA Modules:
  0.0 85.2 jit_solution(1860086588183862484)
XLA Ops:
  0.6 0.0 copy-start.2
  0.7 0.6 copy-done.2
  1.3 0.7 select_reduce_fusion.inv
  2.0 79.3 %shard_map.76 = (bf16[2,64,4096]{2,1,0:T(8,128)(2,1)}, bf16[2,64,512]{2,1,0:T(8,128)(2,1)}, bf16[2,64,512]{2,1,0:T(8,128)(2,1)}) custom-call(s32[256]{0:T(256)} %select_reduce_fusion.inv, s32[256]{0:T(256)} %bp.1, bf16[2,64,4096]{2,1,0:T(8,128)(2,1)} %bitcast.6, bf16[2,64,512]{2,1,0:T(8,128)(2,1)} %bitcast.8, bf16[2,64,512]{2,1,0:T(8,128)(2,1)} %bitcast.9), custom_call_target="tpu_custom_call" | custom-call | tf_op jit(solution)/shard_map/pallas_call | solution.py:398
  81.2 0.0 copy-start.1
  81.3 2.3 %copy.11 = bf16[128,4096]{1,0:T(8,128)(2,1)} copy(bf16[128,4096]{1,0:T(8,128)(2,1)} %bitcast.7) | data formatting | bytes 2097152
  83.6 0.0 copy-done.1
  83.6 0.0 copy-start
  83.6 0.7 copy.12
  84.2 0.3 copy-done
  84.5 0.7 copy.13
  (1 shorter events, 0.0 us)
Async XLA Ops:
  0.6 0.7 copy-start.2
  81.2 2.3 %copy-start.1 = (bf16[2,64,512]{2,1,0:T(8,128)(2,1)S(1)}, bf16[2,64,512]{2,1,0:T(8,128)(2,1)}, u32[]{:S(2)}) copy-start(bf16[2,64,512]{2,1,0:T(8,128)(2,1)} %get-tuple-element.7) | copy-start | bytes 393220
  83.6 1.0 %copy-start = (bf16[2,64,512]{2,1,0:T(8,128)(2,1)S(1)}, bf16[2,64,512]{2,1,0:T(8,128)(2,1)}, u32[]{:S(2)}) copy-start(bf16[2,64,512]{2,1,0:T(8,128)(2,1)} %get-tuple-element.8) | copy-start | bytes 393220

commit v3 on v2

--- a/solution.py
+++ b/solution.py
@@ -231,11 +231,13 @@
         return jnp.concatenate([kv[pl.ds(b, 2), a, 0].reshape(2 * HALF, HEAD) for b in base], axis=0)
 
     def dense_scores(n, base, s):
-        put_scores(n, dot_scores(early_rows(base, 0), q2[s, :, HEAD:]))
+        s_new = dot_scores(early_rows(base, 0), q2[s, :, HEAD:])
+        bufs[n][...] = s_new
+        tops[n][0] = jnp.max(s_new.reshape(KEYS // 8, 8, COLS), axis=0)
 
     def dense_sum(n, base, s):
         old = ms[s, 1]
-        new = jnp.maximum(old, jnp.max(jnp.max(tops[n][...], axis=0), axis=0, keepdims=True) * SCALE)
+        new = jnp.maximum(old, jnp.max(tops[n][0], axis=0, keepdims=True) * SCALE)
         fade = jnp.exp2(old - new)
         ms[s, 1] = new
         p = jnp.exp2(bufs[n][...] * SCALE - ms[s, 1])
@@ -341,7 +343,10 @@
         s = (n + 1) * (1 - own)
         pair = 3 * (1 - own) + (n - 3) * own
         both = [chunk(2 * pair), chunk(2 * pair + 1)]
-        run([dense_unit(base, s) for base, _ in both] + [side_unit(base, places, s) for base, places in both])
+        units = []
+        for base, places in both:
+            units += [dense_unit(base, s), side_unit(base, places, s)]
+        run(units)
         @pl.when(own == n // 6)
         def _():
             for e in (0, 1):

time: 85.4 us -> 84.4 us (0.988)
  Pallas kernels: 79.3 us -> 78.3 us
    pallas_call x1, Pallas kernels: 79.3 us -> 78.3 us  [local(): pl.pallas_call(kernel, out_shape=tuple((jax.ShapeDtypeStruct(a.shape, bf)...]
where the time goes in v3:
time: 84.4 us; the launch traced here: 84.2 us
  Pallas kernels  78.3 us (93%)
  local copies, waits for them, and re-layouts  4.58 us (5%)
    pallas_call x1, Pallas kernels, local(): pl.pallas_call(kernel, out_shape=tuple((jax.ShapeDtypeStruct(a.shape, bf)...  78.3 us
    unnamed x9, local copies, waits for them, and re-layouts  4.58 us

profile of v3, /device:TPU:0, one launch (start us, length us, event | category | flops | bytes accessed | tf_op | source)
XLA Modules:
  0.0 84.2 jit_solution(7588170923687043672)
XLA Ops:
  0.6 0.0 copy-start.2
  0.7 0.6 copy-done.2
  1.3 0.7 select_reduce_fusion.inv
  2.0 78.3 %shard_map.76 = (bf16[2,64,4096]{2,1,0:T(8,128)(2,1)}, bf16[2,64,512]{2,1,0:T(8,128)(2,1)}, bf16[2,64,512]{2,1,0:T(8,128)(2,1)}) custom-call(s32[256]{0:T(256)} %select_reduce_fusion.inv, s32[256]{0:T(256)} %bp.1, bf16[2,64,4096]{2,1,0:T(8,128)(2,1)} %bitcast.6, bf16[2,64,512]{2,1,0:T(8,128)(2,1)} %bitcast.8, bf16[2,64,512]{2,1,0:T(8,128)(2,1)} %bitcast.9), custom_call_target="tpu_custom_call" | custom-call | tf_op jit(solution)/shard_map/pallas_call | solution.py:403
  80.3 0.0 copy-start.1
  80.3 2.3 %copy.11 = bf16[128,4096]{1,0:T(8,128)(2,1)} copy(bf16[128,4096]{1,0:T(8,128)(2,1)} %bitcast.7) | data formatting | bytes 2097152
  82.6 0.0 copy-done.1
  82.6 0.0 copy-start
  82.6 0.7 copy.12
  83.3 0.3 copy-done
  83.6 0.7 copy.13
  (1 shorter events, 0.0 us)
Async XLA Ops:
  0.6 0.7 copy-start.2
  80.3 2.3 %copy-start.1 = (bf16[2,64,512]{2,1,0:T(8,128)(2,1)S(1)}, bf16[2,64,512]{2,1,0:T(8,128)(2,1)}, u32[]{:S(2)}) copy-start(bf16[2,64,512]{2,1,0:T(8,128)(2,1)} %get-tuple-element.7) | copy-start | bytes 393220
  82.6 1.0 %copy-start = (bf16[2,64,512]{2,1,0:T(8,128)(2,1)S(1)}, bf16[2,64,512]{2,1,0:T(8,128)(2,1)}, u32[]{:S(2)}) copy-start(bf16[2,64,512]{2,1,0:T(8,128)(2,1)} %get-tuple-element.8) | copy-start | bytes 393220
